TPU v7x, 128 devices: a whole 4x4x4 slice. The times are simulated.
128 devices in a mesh: mem: 16 (over y, x), reg: 8 (over z, core).
Axes of the slice: x: 4, y: 4, z: 4, core: 2. Of those that a mesh axis runs over, the one named last changes fastest.
Arguments:
- prior_samples: bfloat16 [1024, 16, 8, 1920], P('mem', None, 'reg'), may hold values from -7 to 7
- measured_anomalies: bfloat16 [16, 8, 2048, 1024], P('mem', 'reg'), may hold values from -6 to 6
- measured_departure: bfloat16 [16, 8, 2048], P('mem', 'reg'), may hold values from -6 to 6
- measure_inverse_variance: bfloat16 [16, 8, 2048], P('mem', 'reg'), may hold values from 0.25 to 4
- measure_neighbour_code: int32 [16, 8, 2560], P('mem', 'reg'), may hold values from 0 to 2
- measure_position: int32 [16, 8, 2560], P('mem', 'reg'), may hold values from 0 to 2047, as said below
- measure_tally: int32 [16, 8], P('mem', 'reg'), may hold values from 1280 to 2560, as said below
- locality_weights: float32 [16, 8, 2560], P('mem', 'reg'), may hold values from 0.1 to 1
Outputs:
- analysis: bfloat16 [1024, 16, 8, 1920], P('mem', None, 'reg')
Inputs may be any that keep to these rules, and one draw needn't show every extreme that they name: `measure_position`: an entry with measure_neighbour_code 0 names one of the last 512 rows of its block, one with measure_neighbour_code 2 one of the first 512; the 2560 entries of one block's list name distinct observations. `measure_tally`: some block uses all 2560 entries and some block exactly 1280.
All inputs are finite; a program needn't handle non-finite values.
Results may differ from a plain program's by a relative error of at most 0.0017.
The roundings to bfloat16 on the way count: a program that leaves them out, or rounds other values in their place, can miss the bound.
Values may be sent and summed in bfloat16 or wider, within the bound.
A program may use at most 128 MiB of HBM per device.

v0:
```python
import jax
import jax.numpy as jnp
from jax import lax
from jax.sharding import PartitionSpec as P

inflation = 1.1


def from_behind(block, axis, distance):
    devices = range(lax.axis_size(axis))
    route = [((i - distance) % len(devices), i) for i in devices]
    return lax.ppermute(block, axis, route)


def top_dot(left, right):
    return jnp.dot(left, right, precision=lax.Precision.HIGHEST)


def transform_matrix(picked, weight, innov_picked):
    sample_total = picked.shape[1]
    scaled = (picked.astype(jnp.float32) * weight[:, None]).astype(jnp.bfloat16)
    gram_matrix = lax.dot_general(
        scaled, picked, (((0,), (0,)), ((), ())), preferred_element_type=jnp.float32
    )
    forcing = (weight * innov_picked).astype(jnp.bfloat16)
    drive_vec = jnp.dot(forcing, picked, preferred_element_type=jnp.float32)
    identity = jnp.eye(sample_total, dtype=jnp.float32)
    system = gram_matrix + (sample_total - 1) / inflation * identity
    probe_vec = jnp.ones((sample_total,), jnp.float32)
    for iteration in range(6):
        probe_vec = top_dot(system, probe_vec)
        probe_vec = probe_vec / jnp.sqrt(jnp.sum(probe_vec * probe_vec))
    bound_val = jnp.sum(probe_vec * top_dot(system, probe_vec))
    unit_sys = system / bound_val
    first_step = (3.0 * identity - unit_sys) * 0.5
    second = (3.0 * identity - top_dot(first_step, top_dot(unit_sys, first_step))) * 0.5
    root_inv = top_dot(second, first_step)
    mean_weights = top_dot(root_inv, top_dot(root_inv, drive_vec)) / bound_val
    return (jnp.sqrt((sample_total - 1) / bound_val) * root_inv + mean_weights[:, None]).astype(
        jnp.bfloat16
    )


def apply_transform(ensemble_transform, grid_width):
    sample_total = grid_width.shape[0]
    center = jnp.sum(grid_width, axis=0, dtype=jnp.float32) / sample_total
    deviation = (grid_width.astype(jnp.float32) - center).astype(jnp.bfloat16)
    moved = lax.dot_general(
        ensemble_transform, deviation, (((0,), (0,)), ((), ())), preferred_element_type=jnp.float32
    )
    return (center + moved).astype(jnp.bfloat16)


def local(
    prior_samples,
    measured_anomalies,
    measured_departure,
    measure_inverse_variance,
    measure_neighbour_code,
    measure_position,
    measure_tally,
    locality_weights,
):
    obs_rows = measured_anomalies[0, 0]
    own_innov = measured_departure[0, 0]
    own_prec = measure_inverse_variance[0, 0]
    obs_total = obs_rows.shape[0]
    side_code = measure_neighbour_code[0, 0]
    slot_code = measure_position[0, 0]
    before = from_behind((obs_rows, own_innov, own_prec), ("mem", "reg"), 1)
    following = from_behind((obs_rows, own_innov, own_prec), ("mem", "reg"), -1)
    window_index = side_code * obs_total + slot_code
    window_rows = jnp.concatenate([before[0], obs_rows, following[0]], axis=0)
    window_innov = jnp.concatenate([before[1], own_innov, following[1]], axis=0)
    window_prec = jnp.concatenate([before[2], own_prec, following[2]], axis=0)
    picked = jnp.take(window_rows, window_index, axis=0)
    live = jnp.arange(side_code.shape[0], dtype=jnp.int32) < measure_tally[0, 0]
    weight = jnp.where(
        live,
        jnp.take(window_prec, window_index).astype(jnp.float32) * locality_weights[0, 0],
        jnp.float32(0.0),
    )
    innov_picked = jnp.take(window_innov, window_index).astype(jnp.float32)
    ensemble_transform = transform_matrix(picked, weight, innov_picked)
    analysed = apply_transform(
        ensemble_transform,
        lax.all_to_all(prior_samples, "mem", split_axis=1, concat_axis=0, tiled=True)[:, 0, 0, :],
    )[:, None, None, :]
    return lax.all_to_all(analysed, "mem", split_axis=0, concat_axis=1, tiled=True)


def solution(mesh):
    return jax.shard_map(
        local,
        mesh=mesh,
        in_specs=(
            P("mem", None, "reg", None),
            P("mem", "reg", None, None),
            P("mem", "reg", None),
            P("mem", "reg", None),
            P("mem", "reg", None),
            P("mem", "reg", None),
            P("mem", "reg"),
            P("mem", "reg", None),
        ),
        out_specs=P("mem", None, "reg", None),
        check_vma=False,
    )
```

profile of v0, /device:TPU:0, one launch (start us, length us, event | category | flops | bytes accessed | tf_op | source)
XLA Modules:
  0.0 408.2 jit_solution(1101123496069496911)
XLA Ops:
  0.0 4.9 %copy.21 = bf16[64,16,1,1920]{3,0,2,1:T(8,128)(2,1)} copy(bf16[64,16,1,1920]{3,1,2,0:T(8,128)(2,1)} %param.10) | data formatting | bytes 7864320 | tf_op args[0]
  4.9 7.3 %all-to-all-start = ((bf16[64,16,1,1920]{3,0,2,1:T(8,128)(2,1)}), bf16[64,16,1,1920]{3,0,2,1:T(8,128)(2,1)}, u32[]{:S(2)}, u32[]{:S(2)}) async-start(bf16[64,16,1,1920]{3,0,2,1:T(8,128)(2,1)} %copy.21), calls=%async_computation | async-start | bytes 7864320 | tf_op jit(solution)/shard_map/all_to_all | solution.py:87
  12.2 0.1 collective-permute-start
  12.3 7.6 %collective-permute-start.1 = (bf16[2048,1024]{1,0:T(8,128)(2,1)}, bf16[2048,1024]{1,0:T(8,128)(2,1)}, u32[]{:S(2)}, u32[]{:S(2)}) collective-permute-start(bf16[2048,1024]{1,0:T(8,128)(2,1)} %bitcast.64), channel_id=1, source_target_pairs={{1,0},{2,1},{3,2},{4,3},{5,4},{6,5},{7,6},{8,7},{9,8},{10,9},{11,1... | collective-permute-start | bytes 12582920 | tf_op jit(solution)/shard_map/ppermute | solution.py:12
  19.9 0.1 collective-permute-start.2
  20.0 7.2 %collective-permute-start.3 = (bf16[2048]{0:T(1024)(128)(2,1)S(1)}, bf16[2048]{0:T(1024)(128)(2,1)S(1)}, u32[]{:S(2)}, u32[]{:S(2)}) collective-permute-start(bf16[2048]{0:T(1024)(128)(2,1)S(1)} %reduce.5), channel_id=1, source_target_pairs={{1,0},{2,1},{3,2},{4,3},{5,4},{6,5},{7,6},{8,7},{9,8},{10,9},{11,1... | collective-permute-start | bytes 12296 | tf_op jit(solution)/shard_map/ppermute | solution.py:12
  28.1 86.1 %collective-permute-done.2 = bf16[2048]{0:T(1024)(128)(2,1)S(1)} collective-permute-done((bf16[2048]{0:T(1024)(128)(2,1)S(1)}, bf16[2048]{0:T(1024)(128)(2,1)S(1)}, u32[]{:S(2)}, u32[]{:S(2)}) %collective-permute-start.2) | collective-permute-done | bytes 4128 | tf_op jit(solution)/shard_map/ppermute | solution.py:12
  114.2 0.2 collective-permute-start.5
  114.4 15.4 %gather_fusion.1 = bf16[2560]{0:T(1024)(128)(2,1)S(1)} fusion(bf16[6144]{0:T(1024)(128)(2,1)S(1)} %pad_maximum_fusion.1, s32[3072]{0:T(1024)S(1)} %pad_clamp_fusion), kind=kCustom, calls=%fused_computation.clone | custom fusion | bytes 20480 | tf_op jit(solution)/shard_map/jit(_take)/gather | solution.py:80
  129.8 15.4 %gather_fusion.2 = bf16[2560]{0:T(1024)(128)(2,1)S(1)} fusion(bf16[6144]{0:T(1024)(128)(2,1)S(1)} %pad_maximum_fusion.2, s32[3072]{0:T(1024)S(1)} %pad_clamp_fusion), kind=kCustom, calls=%fused_computation.1.clone | custom fusion | bytes 20480 | tf_op jit(solution)/shard_map/jit(_take)/gather | solution.py:83
  145.3 4.4 %convert_bitcast_fusion = f32[16,64,1,1,1920]{4,0,1,3,2:T(8,128)S(1)} fusion(bf16[64,16,1,1920]{3,0,2,1:T(8,128)(2,1)} %all-to-all-done), kind=kLoop, calls=%fused_computation.5 | loop fusion | flops 1966080 | bytes 11796480 | tf_op jit(solution)/shard_map/convert_element_type | solution.py:46
  149.7 2.5 copy.23
  152.2 4.2 %convert_reduce_fusion = f32[1920]{0:T(1024)S(1)} fusion(bf16[64,16,1,1920]{3,0,2,1:T(8,128)(2,1)} %all-to-all-done), kind=kLoop, calls=%fused_computation.6 | loop fusion | flops 3930240 | bytes 3939840 | tf_op jit(solution)/shard_map/reduce_sum | solution.py:46
  156.4 2.6 fusion.1
  159.0 1.0 copy-done.3
  160.0 10.3 %pad_maximum_fusion = bf16[6144,1024]{1,0:T(8,128)(2,1)} fusion(bf16[2048,1024]{1,0:T(8,128)(2,1)} %collective-permute-done.1, bf16[2048,1024]{1,0:T(8,128)(2,1)S(1)} %bitcast.65, bf16[2048,1024]{1,0:T(8,128)(2,1)} %collective-permute-done), kind=kLoop, calls=%fused_computation.3 | loop fusion | flops 37748736 | bytes 25165824 | tf_op jit(solution)/shard_map/concatenate | solution.py:73
  170.3 18.5 %gather_fusion = bf16[2560,1024]{1,0:T(8,128)(2,1)} fusion(bf16[6144,1024]{1,0:T(8,128)(2,1)} %pad_maximum_fusion, s32[3072]{0:T(1024)S(1)} %pad_clamp_fusion.1), kind=kCustom, calls=%fused_computation.2 | custom fusion | bytes 10496000 | tf_op jit(solution)/shard_map/jit(_take)/gather | solution.py:76
  188.8 10.4 %select_add_fusion = f32[1024,1024]{1,0:T(8,128)S(1)} fusion(bf16[2560,1024]{1,0:T(8,128)(2,1)} %gather_fusion, pred[2560]{0:T(1024)(128)(4,1)S(1)} %get-tuple-element.8, f32[2560]{0:T(1024)S(1)} %get-tuple-element.7), kind=kOutput, calls=%fused_computation.19 | convolution fusion | flops 5384962048 | bytes 9449984 | tf_op jit(solution)/shard_map/dot_general | solution.py:22
  199.2 1.9 copy-done
  201.1 3.6 fusion.27
  204.7 0.6 multiply_reduce_fusion.6
  206.0 5.8 %fusion.42 = f32[1,1024]{1,0:T(1,128)S(1)} fusion(f32[1024,1024]{1,0:T(8,128)} %copy-done, f32[1024,1]{0,1:T(1,128)S(1)} %bitcast.80), kind=kOutput, calls=%fused_computation.81 | convolution fusion | flops 12582912 | bytes 4202496 | tf_op jit(solution)/shard_map/dot_general | solution.py:16
  211.8 0.6 multiply_reduce_fusion.5
  213.1 6.2 %fusion.43 = f32[1,1024]{1,0:T(1,128)S(1)} fusion(f32[1024,1024]{1,0:T(8,128)} %copy-done, f32[1024,1]{0,1:T(1,128)S(1)} %bitcast.81), kind=kOutput, calls=%fused_computation.82 | convolution fusion | flops 12582912 | bytes 4202496 | tf_op jit(solution)/shard_map/dot_general | solution.py:16
  219.2 0.6 multiply_reduce_fusion.4
  220.5 5.8 %fusion.44 = f32[1,1024]{1,0:T(1,128)S(1)} fusion(f32[1024,1024]{1,0:T(8,128)} %copy-done, f32[1024,1]{0,1:T(1,128)S(1)} %bitcast.82), kind=kOutput, calls=%fused_computation.83 | convolution fusion | flops 12582912 | bytes 4202496 | tf_op jit(solution)/shard_map/dot_general | solution.py:16
  226.3 0.6 multiply_reduce_fusion.3
  227.6 5.8 %fusion.45 = f32[1,1024]{1,0:T(1,128)S(1)} fusion(f32[1024,1024]{1,0:T(8,128)} %copy-done, f32[1024,1]{0,1:T(1,128)S(1)} %bitcast.83), kind=kOutput, calls=%fused_computation.84 | convolution fusion | flops 12582912 | bytes 4202496 | tf_op jit(solution)/shard_map/dot_general | solution.py:16
  233.4 0.6 multiply_reduce_fusion.2
  234.7 5.8 %fusion.46 = f32[1,1024]{1,0:T(1,128)S(1)} fusion(f32[1024,1024]{1,0:T(8,128)} %copy-done, f32[1024,1]{0,1:T(1,128)S(1)} %bitcast.84), kind=kOutput, calls=%fused_computation.85 | convolution fusion | flops 12582912 | bytes 4202496 | tf_op jit(solution)/shard_map/dot_general | solution.py:16
  240.4 0.6 multiply_reduce_fusion.1
  241.7 6.1 %fusion.47 = f32[1,1024]{1,0:T(1,128)S(1)} fusion(f32[1024,1024]{1,0:T(8,128)} %copy-done, f32[1024,1]{0,1:T(1,128)S(1)} %bitcast.86), kind=kOutput, calls=%fused_computation.86 | convolution fusion | flops 12582912 | bytes 4202496 | tf_op jit(solution)/shard_map/dot_general | solution.py:16
  247.8 0.6 multiply_reduce_fusion
  248.4 14.6 %fusion.10 = f32[1024,1024]{1,0:T(8,128)S(1)} fusion(f32[1024,1024]{1,0:T(8,128)S(1)} %copy-done.1, f32[]{:T(128)} %multiply_reduce_fusion), kind=kOutput, calls=%fused_computation.22 | convolution fusion | flops 12891193344 | bytes 8388612 | tf_op jit(solution)/shard_map/dot_general | solution.py:16
  263.0 14.8 %fusion.8 = f32[1024,1024]{1,0:T(8,128)S(1)} fusion(f32[1024,1024]{1,0:T(8,128)S(1)} %fusion.10, f32[1024,1024]{1,0:T(8,128)S(1)} %copy-done.1, f32[]{:T(128)} %multiply_reduce_fusion), kind=kOutput, calls=%fused_computation.21 | convolution fusion | flops 12890144768 | bytes 12582916 | tf_op jit(solution)/shard_map/dot_general | solution.py:16
  277.8 14.6 %fusion.5 = f32[1024,1024]{1,0:T(8,128)S(1)} fusion(f32[1024,1024]{1,0:T(8,128)S(1)} %fusion.8, f32[1024,1024]{1,0:T(8,128)S(1)} %copy-done.1, f32[]{:T(128)} %multiply_reduce_fusion), kind=kOutput, calls=%fused_computation.17 | convolution fusion | flops 12894339072 | bytes 12582916 | tf_op jit(solution)/shard_map/dot_general | solution.py:16
  292.4 0.9 fusion.25
  293.3 3.6 convolution_bitcast_fusion
  297.0 3.7 fusion.48
  300.6 0.6 broadcast_divide_fusion.1
  302.0 10.0 %fusion.12 = bf16[1024,1,1,1920]{3,0,2,1:T(8,128)(2,1)} fusion(f32[1920]{0:T(1024)S(1)} %broadcast_multiply_fusion, bf16[1024,1920]{1,0:T(8,128)(2,1)} %fusion.1, f32[1024,1024]{1,0:T(8,128)} %copy-done.2, f32[1024]{0:T(1024)S(1)} %broadcast_divide_fusion.1, f32[]{:T(128)S(6)} %sqrt.27), kind=kOutput, calls=%fused_computation.23 | convolution fusion | flops 4033609728 | bytes 12070404 | tf_op jit(solution)/shard_map/dot_general | solution.py:48
  311.9 0.6 broadcast.121
  312.5 6.7 %reduce.10 = bf16[1024,1920]{1,0:T(8,128)(2,1)} reduce(bf16[1024,1,1,1920]{3,0,2,1:T(8,128)(2,1)} %fusion.12, bf16[]{:T(256)} %broadcast.121), dimensions={1,2}, to_apply=%copy.24.reduce_sub_computation | reduce | bytes 7864322 | tf_op jit(solution)/shard_map/broadcast_in_dim | solution.py:85
  319.2 10.5 %reshape.116 = bf16[16,2,61440]{2,1,0:T(2,128)(2,1)} reshape(bf16[1024,1920]{1,0:T(8,128)(2,1)} %reduce.10) | data formatting | bytes 7864320
  329.7 58.1 %all_to_all.27 = bf16[16,2,61440]{2,1,0:T(2,128)(2,1)} all-to-all(bf16[16,2,61440]{2,1,0:T(2,128)(2,1)} %reshape.116), channel_id=1, replica_groups=mesh['mem'=16,'reg'=8] {'mem'}, dimensions={0} | all-to-all | bytes 7864320 | tf_op jit(solution)/shard_map/all_to_all | solution.py:89
  387.8 12.2 %reshape.117 = bf16[1024,1,1,1920]{3,2,1,0:T(2,128)(2,1)} reshape(bf16[16,2,61440]{2,1,0:T(2,128)(2,1)} %all_to_all.27) | data formatting | bytes 7864320
  400.0 3.8 copy.26
  403.9 4.1 %copy.25 = bf16[64,16,1,1920]{3,1,2,0:T(8,128)(2,1)} copy(bf16[64,16,1,1920]{3,0,1,2:T(8,128)(2,1)S(1)} %bitcast.60) | data formatting | bytes 7864320 | tf_op jit(solution)/shard_map/all_to_all | solution.py:89
  (47 shorter events, 0.4 us)
Async XLA Ops:
  4.9 15.0 %copy-start.7 = (bf16[1,1,2048]{2,1,0:T(2,128)(2,1)S(1)}, bf16[1,1,2048]{2,1,0:T(2,128)(2,1)}, u32[]{:S(2)}) copy-start(bf16[1,1,2048]{2,1,0:T(2,128)(2,1)} %param.13) | copy-start | bytes 12292
  4.9 22.3 %copy-start.8 = (bf16[1,1,2048]{2,1,0:T(2,128)(2,1)S(1)}, bf16[1,1,2048]{2,1,0:T(2,128)(2,1)}, u32[]{:S(2)}) copy-start(bf16[1,1,2048]{2,1,0:T(2,128)(2,1)} %param.12) | copy-start | bytes 12292
  4.9 22.4 %copy-start.4 = (s32[1,1,2560]{2,1,0:T(1,128)S(1)}, s32[1,1,2560]{2,1,0:T(1,128)}, u32[]{:S(2)}) copy-start(s32[1,1,2560]{2,1,0:T(1,128)} %param.15) | copy-start | bytes 30724
  4.9 22.4 %copy-start.5 = (s32[1,1,2560]{2,1,0:T(1,128)S(1)}, s32[1,1,2560]{2,1,0:T(1,128)}, u32[]{:S(2)}) copy-start(s32[1,1,2560]{2,1,0:T(1,128)} %param.14) | copy-start | bytes 30724
  4.9 23.2 %copy-start.6 = (f32[1,1,2560]{2,1,0:T(1,128)S(1)}, f32[1,1,2560]{2,1,0:T(1,128)}, u32[]{:S(2)}) copy-start(f32[1,1,2560]{2,1,0:T(1,128)} %param.17) | copy-start | bytes 30724
  4.9 140.3 %all-to-all-start = ((bf16[64,16,1,1920]{3,0,2,1:T(8,128)(2,1)}), bf16[64,16,1,1920]{3,0,2,1:T(8,128)(2,1)}, u32[]{:S(2)}, u32[]{:S(2)}) async-start(bf16[64,16,1,1920]{3,0,2,1:T(8,128)(2,1)} %copy.21), calls=%async_computation | async-start | bytes 7864320 | tf_op jit(solution)/shard_map/all_to_all | solution.py:87
  12.2 146.8 %collective-permute-start = (bf16[2048,1024]{1,0:T(8,128)(2,1)}, bf16[2048,1024]{1,0:T(8,128)(2,1)}, u32[]{:S(2)}, u32[]{:S(2)}) collective-permute-start(bf16[2048,1024]{1,0:T(8,128)(2,1)} %bitcast.63), channel_id=1, source_target_pairs={{127,0},{0,1},{1,2},{2,3},{3,4},{4,5},{5,6},{6,7},{7,8},{8,9},{9,1... | collective-permute-start | bytes 12582920 | tf_op jit(solution)/shard_map/ppermute | solution.py:12
  12.3 146.7 %collective-permute-start.1 = (bf16[2048,1024]{1,0:T(8,128)(2,1)}, bf16[2048,1024]{1,0:T(8,128)(2,1)}, u32[]{:S(2)}, u32[]{:S(2)}) collective-permute-start(bf16[2048,1024]{1,0:T(8,128)(2,1)} %bitcast.64), channel_id=1, source_target_pairs={{1,0},{2,1},{3,2},{4,3},{5,4},{6,5},{7,6},{8,7},{9,8},{10,9},{11,1... | collective-permute-start | bytes 12582920 | tf_op jit(solution)/shard_map/ppermute | solution.py:12
  19.9 94.3 %collective-permute-start.2 = (bf16[2048]{0:T(1024)(128)(2,1)S(1)}, bf16[2048]{0:T(1024)(128)(2,1)S(1)}, u32[]{:S(2)}, u32[]{:S(2)}) collective-permute-start(bf16[2048]{0:T(1024)(128)(2,1)S(1)} %reduce.5), channel_id=1, source_target_pairs={{127,0},{0,1},{1,2},{2,3},{3,4},{4,5},{5,6},{6,7},{7,8},{8,9},{9,1... | collective-permute-start | bytes 12296 | tf_op jit(solution)/shard_map/ppermute | solution.py:12
  20.0 94.4 %collective-permute-start.3 = (bf16[2048]{0:T(1024)(128)(2,1)S(1)}, bf16[2048]{0:T(1024)(128)(2,1)S(1)}, u32[]{:S(2)}, u32[]{:S(2)}) collective-permute-start(bf16[2048]{0:T(1024)(128)(2,1)S(1)} %reduce.5), channel_id=1, source_target_pairs={{1,0},{2,1},{3,2},{4,3},{5,4},{6,5},{7,6},{8,7},{9,8},{10,9},{11,1... | collective-permute-start | bytes 12296 | tf_op jit(solution)/shard_map/ppermute | solution.py:12
  27.2 102.6 %collective-permute-start.4 = (bf16[2048]{0:T(1024)(128)(2,1)S(1)}, bf16[2048]{0:T(1024)(128)(2,1)S(1)}, u32[]{:S(2)}, u32[]{:S(2)}) collective-permute-start(bf16[2048]{0:T(1024)(128)(2,1)S(1)} %reduce.7), channel_id=1, source_target_pairs={{127,0},{0,1},{1,2},{2,3},{3,4},{4,5},{5,6},{6,7},{7,8},{8,9},{9,1... | collective-permute-start | bytes 12296 | tf_op jit(solution)/shard_map/ppermute | solution.py:12
  114.2 15.6 %collective-permute-start.5 = (bf16[2048]{0:T(1024)(128)(2,1)S(1)}, bf16[2048]{0:T(1024)(128)(2,1)S(1)}, u32[]{:S(2)}, u32[]{:S(2)}) collective-permute-start(bf16[2048]{0:T(1024)(128)(2,1)S(1)} %reduce.7), channel_id=1, source_target_pairs={{1,0},{2,1},{3,2},{4,3},{5,4},{6,5},{7,6},{8,7},{9,8},{10,9},{11,1... | collective-permute-start | bytes 12296 | tf_op jit(solution)/shard_map/ppermute | solution.py:12
  156.4 3.6 copy-start.3
  199.2 1.9 copy-start
  241.7 6.7 %copy-start.1 = (f32[1024,1024]{1,0:T(8,128)S(1)}, f32[1024,1024]{1,0:T(8,128)}, u32[]{:S(2)}) copy-start(f32[1024,1024]{1,0:T(8,128)} %copy-done) | copy-start | bytes 12582916
  248.4 44.0 %slice-start = ((s8[5242880]{0:T(1024)(128)(4,1)}), s8[4194304]{0:T(1024)(128)(4,1)S(1)}, s32[]{:S(2)}) async-start(s8[5242880]{0:T(1024)(128)(4,1)} %bitcast.61), calls=%async_computation.2 | async-start | bytes 8388608
  263.0 29.4 %slice-start.1 = ((s8[5242880]{0:T(1024)(128)(4,1)}), s8[1048576]{0:T(1024)(128)(4,1)S(1)}, s32[]{:S(2)}) async-start(s8[5242880]{0:T(1024)(128)(4,1)} %bitcast.61), calls=%async_computation.3 | async-start | bytes 2097152
  292.4 4.5 %copy-start.2 = (f32[1024,1024]{1,0:T(8,128)}, f32[1024,1024]{1,0:T(8,128)S(1)}, u32[]{:S(2)}) copy-start(f32[1024,1024]{1,0:T(8,128)S(1)} %fusion.5) | copy-start | bytes 12582916
where the time goes:
time: 413 us; the launch traced here: 408 us
  matrix products  111 us (27%)
  local copies, waits for them, and re-layouts  90.9 us (22%)
  waiting for transfers between devices  86.1 us (21%)
  blocking collectives  58.1 us (14%)
  other arithmetic  33.4 us (8%)
  starting transfers between devices  22.4 us (5%)
  between operations  5.95 us (1%)
    dot_general x12, matrix products, top_dot(): return jnp.dot(left, right, precision=lax.Precision.HIGHEST)  90.1 us
    ppermute x6, waiting for transfers between devices, from_behind(): return lax.ppermute(block, axis, route)  86.1 us
    all_to_all x1, blocking collectives, local(): lax.all_to_all(analysed, 'mem', split_axis=0, concat_axis=1, tiled=True)  58.1 us
    unnamed x26, local copies, waits for them, and re-layouts  34.4 us
    gather x1, local copies, waits for them, and re-layouts, local(): picked = jnp.take(window_rows, window_index, axis=0)  18.5 us
    gather x1, local copies, waits for them, and re-layouts, local(): jnp.take(window_prec, window_index).astype(jnp.float32)  15.4 us
    gather x1, local copies, waits for them, and re-layouts, local(): innov_picked = jnp.take(window_innov, window_index).astype(jnp.float32)  15.4 us
    ppermute x6, starting transfers between devices, from_behind(): return lax.ppermute(block, axis, route)  15.1 us
  transfers between devices with their start and end apart: 7, of which 1 were waited for; matrix products, arithmetic and copies ran while one was open for 11% of the time, Pallas kernels for 0%

commit v1 on v0

v1 whole, which is shorter than its diff:
```python
import functools

import jax
import jax.numpy as jnp
from jax import lax
from jax.experimental import pallas as pl
from jax.experimental.pallas import tpu as pltpu
from jax.sharding import PartitionSpec as P

MESH = pl.DeviceIdType.MESH
F32, BF16 = jnp.float32, jnp.bfloat16

MEMBERS = 1024
OWN = 2048
RIM = 512
WINDOW = OWN + 2 * RIM
LIST = 2560
GROUP = 16
SHARE = MEMBERS // GROUP
GRID = 1920
PARTS = 5
WIDE = GRID // PARTS
RIDGE = (MEMBERS - 1) / 1.1

PEERS = (
    (0, 1), (1, 0), (0, 3), (3, 0),
    (1, 1), (3, 3), (1, 3), (3, 1),
    (0, 2), (2, 0),
    (1, 2), (2, 1), (3, 2), (2, 3),
    (2, 2),
)
NPEER = len(PEERS)

MID = 0.5
A0 = (36 - 39 * MID + 27 * MID**2 - 9 * MID**3 + MID**4) / 16
A1 = (-39 + 54 * MID - 27 * MID**2 + 4 * MID**3) / 16
A2 = (27 - 27 * MID + 6 * MID**2) / 16
A3 = (-9 + 4 * MID) / 16
A4 = 1 / 16


def dot(left, right):
    return jnp.dot(left, right, preferred_element_type=F32)


def split(value):
    high = value.astype(BF16)
    return high, (value - high.astype(F32)).astype(BF16)


def total(value):
    return jnp.sum(value, axis=(0, 1), keepdims=True)


def eye_tile(row, col, rows, cols):
    return (row + lax.broadcasted_iota(jnp.int32, (rows, cols), 0)) == (
        col + lax.broadcasted_iota(jnp.int32, (rows, cols), 1)
    )


def row_times(mat, row, out):
    def body(c, norm):
        rows = pl.ds(pl.multiple_of(c * 128, 128), 128)
        acc = mat[rows, 0:128] * row[:, 0:128]
        for j in range(1, 8):
            acc += mat[rows, 128 * j : 128 * j + 128] * row[:, 128 * j : 128 * j + 128]
        col = jnp.sum(acc, axis=1, keepdims=True)
        out[rows, :] = jnp.broadcast_to(col, (128, 128))
        return norm + jnp.sum(col * col, axis=0, keepdims=True)

    return lax.fori_loop(0, 8, body, jnp.zeros((1, 1), F32))


def col_times(mat, col):
    def body(c, acc):
        rows = pl.ds(pl.multiple_of(c * 128, 128), 128)
        x = col[rows, :]
        return tuple(
            acc[j] + jnp.sum((mat[rows, 128 * j : 128 * j + 128] * x).reshape(16, 8, 128), axis=0)
            for j in range(8)
        )

    acc = lax.fori_loop(0, 8, body, tuple(jnp.zeros((8, 128), F32) for _ in range(8)))
    return jnp.concatenate([jnp.sum(t, axis=0, keepdims=True) for t in acc], axis=1)


def kernel(
    prior, obs, dep, prec, code, position, tally, local,
    out,
    stage, send, recv, window, turned, scaled, gram, root, trans, dev,
    temp, listed, weight, innov, column, force, rim_out, rim_in, center,
    load_sem, own_sem, obs_sem, rim_ss, rim_rs, vec_ss, vec_rs, fs, fr, bs, br, back_sem,
):
    a, b = lax.axis_index("mem"), lax.axis_index("reg")
    y, x = a // 4, a % 4

    def peer(k, sign=1):
        dy, dx = PEERS[k]
        return (((y + 4 + sign * dy) % 4) * 4 + (x + 4 + sign * dx) % 4, b)

    after = ((a + (b + 1) // 8) % GROUP, (b + 1) % 8)
    before = ((a + 15 + (b + 7) // 8) % GROUP, (b + 7) % 8)

    def lanes(c):
        return pl.ds(pl.multiple_of(c * WIDE, 128), WIDE)

    def load(c):
        slot = lax.rem(c, 2)
        return pltpu.make_async_copy(prior.at[:, :, lanes(c)], stage.at[slot], load_sem.at[slot])

    def member_rows(d):
        return pl.ds(pl.multiple_of(d * SHARE, SHARE), SHARE)

    def forward(c, k):
        to = peer(k)
        return pltpu.make_async_remote_copy(
            src_ref=send.at[c, member_rows(to[0]), :],
            dst_ref=recv.at[c, member_rows(a), :],
            send_sem=fs.at[c, k], recv_sem=fr.at[c, k],
            device_id=to, device_id_type=MESH,
        )

    def forward_own(c):
        return pltpu.make_async_copy(
            send.at[c, member_rows(a), :], recv.at[c, member_rows(a), :], own_sem.at[c]
        )

    def backward(c, k):
        to = peer(k)
        return pltpu.make_async_remote_copy(
            src_ref=send.at[c, member_rows(to[0]), :],
            dst_ref=out.at[a, :, lanes(c)],
            send_sem=bs.at[c, k], recv_sem=br.at[c, k],
            device_id=to, device_id_type=MESH,
        )

    def backward_own(c):
        return pltpu.make_async_copy(
            send.at[c, member_rows(a), :], out.at[a, :, lanes(c)], back_sem.at[c]
        )

    load(0).start()
    load(1).start()
    own_rows = pltpu.make_async_copy(obs, window.at[pl.ds(0, OWN), :], obs_sem)
    own_rows.start()

    barrier = pltpu.get_barrier_semaphore()
    for k in range(NPEER):
        pl.semaphore_signal(barrier, inc=1, device_id=peer(k), device_id_type=MESH)
    for d in (after, before):
        pl.semaphore_signal(barrier, inc=1, device_id=d, device_id_type=MESH)

    for side, first in ((0, 0), (1, 12)):
        rim_out[side, 0:4, :] = prec[first : first + 4, :]
        rim_out[side, 4:8, :] = dep[first : first + 4, :]
    weight[...] = jnp.zeros_like(weight)
    force[...] = jnp.zeros_like(force)
    innov[0:16, :] = dep[...]

    pl.semaphore_wait(barrier, NPEER + 2)

    rims = []
    for side, first, to in ((0, 0, before), (1, OWN - RIM, after)):
        where = OWN + RIM * (1 - side)
        rims.append((
            pltpu.make_async_remote_copy(
                src_ref=rim_out.at[side], dst_ref=rim_in.at[1 - side],
                send_sem=vec_ss.at[side], recv_sem=vec_rs.at[side],
                device_id=to, device_id_type=MESH,
            ),
            pltpu.make_async_remote_copy(
                src_ref=obs.at[pl.ds(first, RIM), :], dst_ref=window.at[pl.ds(where, RIM), :],
                send_sem=rim_ss.at[side], recv_sem=rim_rs.at[side],
                device_id=to, device_id_type=MESH,
            ),
        ))
    for small, large in rims:
        small.start()
        large.start()

    def send_part(c, _):
        load(c).wait()
        slot = lax.rem(c, 2)

        def shuffle(g, _):
            rows = pl.ds(pl.multiple_of(g * 16, 16), 16)
            for j in range(WIDE // 128):
                cols = slice(128 * j, 128 * j + 128)
                temp[j] = stage[slot, rows, :, cols].astype(F32).reshape(256, 128)
            for j in range(WIDE // 128):
                cols = slice(128 * j, 128 * j + 128)
                for i in range(16):
                    to_rows = pl.ds(pl.multiple_of(i * SHARE + g * 16, 16), 16)
                    send[c, to_rows, cols] = temp[j, pl.ds(i, 16, stride=16), :].astype(BF16)
            return _

        lax.fori_loop(0, SHARE // 16, shuffle, 0)
        for k in range(NPEER):
            forward(c, k).start()
        forward_own(c).start()

        @pl.when(c < PARTS - 2)
        def next_load():
            load(c + 2).start()

        return _

    lax.fori_loop(0, PARTS, send_part, 0)

    listed[...] = jnp.zeros_like(listed)
    live = tally[0, 0]

    def place(e, _):
        cols = pl.ds(pl.multiple_of(e * 512, 512), 512)
        entry = e * 512 + lax.broadcasted_iota(jnp.int32, (1, 512), 1)
        which, pos = code[:, cols], position[:, cols]
        row = jnp.where(which == 1, pos, jnp.where(which == 0, pos + RIM, pos + OWN + RIM))
        high, low = row // 128, row % 128
        value = jnp.where(entry < live, local[:, cols], 0.0)
        one = value.astype(BF16).astype(F32)
        two = (value - one).astype(BF16).astype(F32)
        three = value - one - two
        hot_low = (lax.broadcasted_iota(jnp.int32, (128, 512), 0) == low).astype(F32).astype(BF16)
        hot_high = lax.broadcasted_iota(jnp.int32, (32, 512), 0) == high
        for term in (three, two, one):
            part = jnp.where(hot_high, term, 0.0).astype(BF16)
            listed[...] += lax.dot_general(
                part, hot_low, (((1,), (1,)), ((), ())), preferred_element_type=F32
            )
        return _

    lax.fori_loop(0, LIST // 512, place, 0)

    def rows_ready(first, last):
        force_rows = (weight[first:last, :] * innov[first:last, :]).astype(BF16).astype(F32)
        for h in range(first, last):
            force[0:1, 128 * h : 128 * h + 128] = force_rows[h - first : h - first + 1, :]

        def block(h, _):
            rows = pl.ds(pl.multiple_of(h * 128, 128), 128)
            w = jnp.broadcast_to(weight[pl.ds(h, 1), :], (128, 128)).T
            for j in range(8):
                cols = slice(128 * j, 128 * j + 128)
                tile = window[rows, cols]
                scaled[rows, cols] = (tile.astype(F32) * w).astype(BF16)
                turned[cols, rows] = tile.T
            return _

        lax.fori_loop(first, last, block, 0)

    def tiles(body):
        def step(t, _):
            m = pl.multiple_of((t // 2) * 256, 256)
            n = pl.multiple_of((t % 2) * 512, 512)
            body(m, n, pl.ds(m, 256), pl.ds(n, 512))
            return _

        lax.fori_loop(0, 8, step, 0)

    weight[0:16, :] = prec[...] * listed[0:16, :]
    own_rows.wait()
    rows_ready(0, 16)

    def gram_own(m, n, rows, cols):
        gram[rows, cols] = dot(turned[rows, 0:OWN], scaled[0:OWN, cols])

    tiles(gram_own)

    for small, large in rims:
        small.wait()
        large.wait()
    for side in range(2):
        at = slice(16 + 4 * side, 20 + 4 * side)
        weight[at, :] = rim_in[side, 0:4, :] * listed[at, :]
        innov[at, :] = rim_in[side, 4:8, :]
    rows_ready(16, 24)

    def gram_rim(m, n, rows, cols):
        ridge = jnp.where(eye_tile(m, n, 256, 512), F32(RIDGE), 0.0)
        gram[rows, cols] += dot(turned[rows, OWN:WINDOW], scaled[OWN:WINDOW, cols]) + ridge

    tiles(gram_rim)
    drive = dot(force[...].astype(BF16), window[...])[0:1, :]

    row = jnp.ones((1, MEMBERS), F32)
    for step in range(3):
        norm = row_times(gram, row, column)
        column[...] = column[...] / jnp.sqrt(norm)
        row = col_times(gram, column)
        row = row / jnp.sqrt(total(row * row))
    row_times(gram, row, column)
    turned_back = jnp.concatenate(
        [column[128 * c : 128 * c + 128, :].T[0:1, :] for c in range(8)], axis=1
    )
    bound = total(row * turned_back)

    v_high, v_low, s_high = (turned.at[:, 1024 * k : 1024 * k + 1024] for k in range(3))
    s_low, q_high, q_low = (scaled.at[1024 * k : 1024 * k + 1024, :] for k in range(3))
    inverse = 1.0 / bound

    def shift(m, n, rows, cols):
        v = gram[rows, cols] * inverse - jnp.where(eye_tile(m, n, 256, 512), F32(MID), 0.0)
        gram[rows, cols] = v
        v_high[rows, cols], v_low[rows, cols] = split(v)

    tiles(shift)

    def square(m, n, rows, cols):
        s = dot(v_high[rows, :], v_low[:, cols]) + dot(v_low[rows, :], v_high[:, cols])
        s += dot(v_high[rows, :], v_high[:, cols])
        v = gram[rows, cols]
        s_high[rows, cols], s_low[rows, cols] = split(s)
        q_high[rows, cols], q_low[rows, cols] = split(A3 * v + A4 * s)
        root[rows, cols] = (
            jnp.where(eye_tile(m, n, 256, 512), F32(A0), 0.0) + A1 * v + A2 * s
        )

    tiles(square)

    def quartic(m, n, rows, cols):
        r = dot(s_high[rows, :], q_low[:, cols]) + dot(s_low[rows, :], q_high[:, cols])
        root[rows, cols] += r + dot(s_high[rows, :], q_high[:, cols])

    tiles(quartic)

    row_times(root, drive, column)
    mean = col_times(root, column) * inverse
    size = jnp.sqrt((MEMBERS - 1) * inverse)

    def finish(m, _):
        rows = pl.ds(pl.multiple_of(m * 128, 128), 128)
        trans[rows, :] = (root[rows, :] * size + mean).astype(BF16)
        return _

    lax.fori_loop(0, 8, finish, 0)

    def apply_part(c, _):
        for k in range(NPEER):
            forward(c, k).wait()
        forward_own(c).wait()

        def add(g, acc):
            rows = pl.ds(pl.multiple_of(g * 128, 128), 128)
            return acc + jnp.sum(recv[c, rows, :].astype(F32).reshape(16, 8, WIDE), axis=0)

        acc = lax.fori_loop(0, 8, add, jnp.zeros((8, WIDE), F32))
        center[...] = jnp.sum(acc, axis=0, keepdims=True) / MEMBERS

        def deviate(g, _):
            rows = pl.ds(pl.multiple_of(g * 128, 128), 128)
            dev[rows, :] = (recv[c, rows, :].astype(F32) - center[...]).astype(BF16)
            return _

        lax.fori_loop(0, 8, deviate, 0)

        def multiply(g, _):
            rows = pl.ds(pl.multiple_of(g * 256, 256), 256)
            send[c, rows, :] = (center[...] + dot(trans[rows, :], dev[...])).astype(BF16)
            return _

        lax.fori_loop(0, 4, multiply, 0)
        for k in range(NPEER):
            backward(c, k).start()
        backward_own(c).start()
        return _

    lax.fori_loop(0, PARTS, apply_part, 0)

    def drain(c, _):
        for k in range(NPEER):
            backward(c, k).wait()
        backward_own(c).wait()
        return _

    lax.fori_loop(0, PARTS, drain, 0)


def local(
    prior_samples,
    measured_anomalies,
    measured_departure,
    measure_inverse_variance,
    measure_neighbour_code,
    measure_position,
    measure_tally,
    locality_weights,
):
    hbm = pl.BlockSpec(memory_space=pl.ANY)
    vmem = pl.BlockSpec(memory_space=pltpu.VMEM)
    smem = pl.BlockSpec(memory_space=pltpu.SMEM)
    dma = pltpu.SemaphoreType.DMA
    moved = pl.pallas_call(
        kernel,
        out_shape=jax.ShapeDtypeStruct((GROUP, SHARE, GRID), BF16),
        in_specs=[hbm, hbm, vmem, vmem, vmem, vmem, smem, vmem],
        out_specs=hbm,
        scratch_shapes=[
            pltpu.VMEM((2, SHARE, GROUP, WIDE), BF16),
            pltpu.VMEM((PARTS, MEMBERS, WIDE), BF16),
            pltpu.VMEM((PARTS, MEMBERS, WIDE), BF16),
            pltpu.VMEM((WINDOW, MEMBERS), BF16),
            pltpu.VMEM((MEMBERS, WINDOW), BF16),
            pltpu.VMEM((WINDOW, MEMBERS), BF16),
            pltpu.VMEM((MEMBERS, MEMBERS), F32),
            pltpu.VMEM((MEMBERS, MEMBERS), F32),
            pltpu.VMEM((MEMBERS, MEMBERS), BF16),
            pltpu.VMEM((MEMBERS, WIDE), BF16),
            pltpu.VMEM((WIDE // 128, 256, 128), F32),
            pltpu.VMEM((32, 128), F32),
            pltpu.VMEM((24, 128), F32),
            pltpu.VMEM((24, 128), F32),
            pltpu.VMEM((MEMBERS, 128), F32),
            pltpu.VMEM((16, WINDOW), F32),
            pltpu.VMEM((2, 8, 128), F32),
            pltpu.VMEM((2, 8, 128), F32),
            pltpu.VMEM((1, WIDE), F32),
            dma((2,)), dma((PARTS,)), dma,
            dma((2,)), dma((2,)), dma((2,)), dma((2,)),
            dma((PARTS, NPEER)), dma((PARTS, NPEER)), dma((PARTS, NPEER)), dma((PARTS, NPEER)),
            dma((PARTS,)),
        ],
        compiler_params=pltpu.CompilerParams(
            collective_id=0, has_side_effects=True, vmem_limit_bytes=58 * 2**20
        ),
        cost_estimate=pl.CostEstimate(flops=24 * 10**9, bytes_accessed=12 * 2**20, transcendentals=0),
    )(
        prior_samples[:, :, 0, :],
        measured_anomalies[0, 0],
        measured_departure[0, 0].astype(F32).reshape(16, 128),
        measure_inverse_variance[0, 0].astype(F32).reshape(16, 128),
        measure_neighbour_code[0],
        measure_position[0],
        measure_tally,
        locality_weights[0],
    )
    return moved.transpose(1, 0, 2)[:, :, None, :]


def solution(mesh):
    return jax.shard_map(
        local,
        mesh=mesh,
        in_specs=(
            P("mem", None, "reg", None),
            P("mem", "reg", None, None),
            P("mem", "reg", None),
            P("mem", "reg", None),
            P("mem", "reg", None),
            P("mem", "reg", None),
            P("mem", "reg"),
            P("mem", "reg", None),
        ),
        out_specs=P("mem", None, "reg", None),
        check_vma=False,
    )
```

time: 413 us -> 118 us (0.29)
  matrix products: 111 us -> 0 us
  Pallas kernels: 0 us -> 107 us
  waiting for transfers between devices: 86.1 us -> 0 us
  local copies, waits for them, and re-layouts: 90.9 us -> 6.21 us
  blocking collectives: 58.1 us -> 0 us
  other arithmetic: 33.4 us -> 2.59 us
  starting transfers between devices: 22.4 us -> 0 us
  between operations: 5.95 us -> 0.66 us
    dot_general x15 -> x0, matrix products: 111 us -> none  [the longest x12 90.1 us: top_dot(): return jnp.dot(left, right, precision=lax.Precision.HIGHEST)]
    pallas_call x0 -> x1, Pallas kernels: none -> 107 us  [local(): pl.pallas_call(kernel, out_shape=jax.ShapeDtypeStruct((GROUP, SHARE, GRID...]
    ppermute x6 -> x0, waiting for transfers between devices: 86.1 us -> none  [from_behind(): return lax.ppermute(block, axis, route)]
    all_to_all x1 -> x0, blocking collectives: 58.1 us -> none  [local(): lax.all_to_all(analysed, 'mem', split_axis=0, concat_axis=1, tiled=True)]
    gather x3 -> x0, local copies, waits for them, and re-layouts: 49.3 us -> none  [the longest x1 18.5 us: local(): picked = jnp.take(window_rows, window_index, axis=0)]
    unnamed x26 -> x0, local copies, waits for them, and re-layouts: 34.4 us -> none
    ppermute x6 -> x0, starting transfers between devices: 15.1 us -> none  [from_behind(): return lax.ppermute(block, axis, route)]
    concatenate x3 -> x0, other arithmetic: 10.3 us -> none  [the longest x1 10.3 us: local(): window_rows = jnp.concatenate([before[0], obs_rows, following[0]], axis=0)]
  transfers between devices with their start and end apart: 7 -> 0, of which waited for: 1 -> 0; matrix products, arithmetic and copies ran while one was open for 11% -> 0% of each run, Pallas kernels for 0% -> 0%
where the time goes in v1:
time: 118 us; the launch traced here: 117 us
  Pallas kernels  107 us (91%)
  local copies, waits for them, and re-layouts  6.21 us (5%)
  other arithmetic  2.59 us (2%)
    pallas_call x1, Pallas kernels, local(): pl.pallas_call(kernel, out_shape=jax.ShapeDtypeStruct((GROUP, SHARE, GRID...  107 us
    broadcast_in_dim x1, local copies, waits for them, and re-layouts, local(): return moved.transpose(1, 0, 2)[:, :, None, :]  6.21 us

profile of v1, /device:TPU:0, one launch (start us, length us, event | category | flops | bytes accessed | tf_op | source)
XLA Modules:
  0.0 116.8 jit_solution(7356489099032567751)
XLA Ops:
  0.7 1.3 %convert_element_type.18 = f32[1,1,2048]{2,1,0:T(1,128)} convert(bf16[1,1,2048]{2,1,0:T(2,128)(2,1)} %param.10) | non-fusion elementwise | flops 2048 | bytes 12288 | tf_op jit(solution)/shard_map/convert_element_type | solution.py:429
  2.0 1.3 %convert_element_type.19 = f32[1,1,2048]{2,1,0:T(1,128)} convert(bf16[1,1,2048]{2,1,0:T(2,128)(2,1)} %param.11) | non-fusion elementwise | flops 2048 | bytes 12288 | tf_op jit(solution)/shard_map/convert_element_type | solution.py:430
  3.2 107.3 %shard_map.82 = bf16[16,64,1920]{2,1,0:T(8,128)(2,1)} custom-call(bf16[64,16,1920]{2,1,0:T(8,128)(2,1)} %bitcast.14, bf16[2048,1024]{1,0:T(8,128)(2,1)} %bitcast.13, f32[16,128]{1,0:T(8,128)} %bitcast.11, f32[16,128]{1,0:T(8,128)} %bitcast.12, s32[1,2560]{1,0:T(1,128)} %bitcast.15, s32[1,2560]{1,0:T(1,128)} %bitcast.16, s32[1,1]{1,0:T(1,128)S(6)} %copy.10.tally, ...), custom_call_target="tpu_custom_call" | custom-call | flops 24000000000 | bytes 12582912 | tf_op jit(solution)/shard_map/pallas_call | solution.py:392
  110.5 6.2 %copy.9 = bf16[64,16,1,1920]{3,1,2,0:T(8,128)(2,1)} copy(bf16[64,16,1,1920]{3,0,1,2:T(8,128)(2,1)} %bitcast.10) | data formatting | bytes 7864320 | tf_op jit(solution)/shard_map/broadcast_in_dim | solution.py:436

commit v2 on v1

v2 whole, which is shorter than its diff:
```python
import functools

import jax
import jax.numpy as jnp
from jax import lax
from jax.experimental import pallas as pl
from jax.experimental.pallas import tpu as pltpu
from jax.sharding import PartitionSpec as P

MESH = pl.DeviceIdType.MESH
F32, BF16 = jnp.float32, jnp.bfloat16

MEMBERS = 1024
OWN = 2048
RIM = 512
WINDOW = OWN + 2 * RIM
LIST = 2560
GROUP = 16
SHARE = MEMBERS // GROUP
GRID = 1920
PARTS = 5
WIDE = GRID // PARTS
RIDGE = (MEMBERS - 1) / 1.1

PEERS = (
    (0, 1), (1, 0), (0, 3), (3, 0),
    (1, 1), (3, 3), (1, 3), (3, 1),
    (0, 2), (2, 0),
    (1, 2), (2, 1), (3, 2), (2, 3),
    (2, 2),
)
NPEER = len(PEERS)

MID = 0.5
A0 = (36 - 39 * MID + 27 * MID**2 - 9 * MID**3 + MID**4) / 16
A1 = (-39 + 54 * MID - 27 * MID**2 + 4 * MID**3) / 16
A2 = (27 - 27 * MID + 6 * MID**2) / 16
A3 = (-9 + 4 * MID) / 16
A4 = 1 / 16


def dot(left, right):
    return jnp.dot(left, right, preferred_element_type=F32)


def split(value):
    high = value.astype(BF16)
    return high, (value - high.astype(F32)).astype(BF16)


def transpose_perm():
    to = lax.broadcasted_iota(jnp.int32, (256, 256), 0)
    source = lax.broadcasted_iota(jnp.int32, (256, 256), 1)
    return jnp.where((to % 16) * 16 + to // 16 == source, 1.0, 0.0).astype(BF16)


def total(value):
    return jnp.sum(value, axis=(0, 1), keepdims=True)


def eye_tile(row, col, rows, cols):
    return (row + lax.broadcasted_iota(jnp.int32, (rows, cols), 0)) == (
        col + lax.broadcasted_iota(jnp.int32, (rows, cols), 1)
    )


def row_times(mat, row, out):
    def body(c, norm):
        rows = pl.ds(pl.multiple_of(c * 128, 128), 128)
        acc = mat[rows, 0:128] * row[:, 0:128]
        for j in range(1, 8):
            acc += mat[rows, 128 * j : 128 * j + 128] * row[:, 128 * j : 128 * j + 128]
        col = jnp.sum(acc, axis=1, keepdims=True)
        out[rows, :] = jnp.broadcast_to(col, (128, 128))
        return norm + jnp.sum(col * col, axis=0, keepdims=True)

    return lax.fori_loop(0, 8, body, jnp.zeros((1, 1), F32))


def to_column(row, out):
    for c in range(8):
        cols = slice(128 * c, 128 * c + 128)
        out[cols, :] = jnp.broadcast_to(row[:, cols], (128, 128)).T


def col_times(mat, col):
    def body(c, acc):
        rows = pl.ds(pl.multiple_of(c * 128, 128), 128)
        x = col[rows, :]
        return tuple(
            acc[j] + jnp.sum((mat[rows, 128 * j : 128 * j + 128] * x).reshape(16, 8, 128), axis=0)
            for j in range(8)
        )

    acc = lax.fori_loop(0, 8, body, tuple(jnp.zeros((8, 128), F32) for _ in range(8)))
    return jnp.concatenate([jnp.sum(t, axis=0, keepdims=True) for t in acc], axis=1)


def kernel(
    prior, obs, dep, prec, code, position, tally, local,
    out,
    stage, send, recv, window, turned, scaled, gram, root, trans, dev, hop, hop_two,
    listed, weight, innov, column, force, rim_out, rim_in, center,
    load_sem, own_sem, obs_sem, hop_sem, rim_ss, rim_rs, vec_ss, vec_rs,
    one_ss, one_rs, two_ss, two_rs, three_ss, three_rs, fs, fr, bs, br, back_sem,
):
    a, b = lax.axis_index("mem"), lax.axis_index("reg")
    y, x = a // 4, a % 4
    plane, odd = b // 2, b % 2
    first_reg, last_reg = b == 0, b == 7

    def peer(k):
        dy, dx = PEERS[k]
        return (((y + dy) % 4) * 4 + (x + dx) % 4, b)

    after = ((a + (b + 1) // 8) % GROUP, (b + 1) % 8)
    before = ((a + 15 + (b + 7) // 8) % GROUP, (b + 7) % 8)
    partner = ((a + 15 + 2 * odd) % GROUP, b + 1 - 2 * odd)

    def remote(src, dst, send_sem, recv_sem, to):
        return pltpu.make_async_remote_copy(
            src_ref=src, dst_ref=dst, send_sem=send_sem, recv_sem=recv_sem,
            device_id=to, device_id_type=MESH,
        )

    def lanes(c):
        return pl.ds(pl.multiple_of(c * WIDE, 128), WIDE)

    def load(c):
        return pltpu.make_async_copy(prior.at[:, :, lanes(c)], stage.at[c], load_sem.at[c])

    def member_rows(d):
        return pl.ds(pl.multiple_of(d * SHARE, SHARE), SHARE)

    def forward(c, k):
        to = peer(k)
        return remote(
            send.at[c, member_rows(to[0]), :], recv.at[c, member_rows(a), :],
            fs.at[c, k], fr.at[c, k], to,
        )

    def forward_own(c):
        return pltpu.make_async_copy(
            send.at[c, member_rows(a), :], recv.at[c, member_rows(a), :], own_sem.at[c]
        )

    def backward(c, k):
        to = peer(k)
        return remote(
            send.at[c, member_rows(to[0]), :], out.at[a, :, lanes(c)], bs.at[c, k], br.at[c, k], to
        )

    def backward_own(c):
        return pltpu.make_async_copy(
            send.at[c, member_rows(a), :], out.at[a, :, lanes(c)], back_sem.at[c]
        )

    barrier = pltpu.get_barrier_semaphore()

    def greet(to):
        pl.semaphore_signal(barrier, inc=1, device_id=to, device_id_type=MESH)

    for k in range(NPEER):
        greet(peer(k))
    for k in range(1, 8):
        greet((a, (b + k) % 8))
    greet(partner)
    pl.when(first_reg)(lambda: greet(before))
    pl.when(last_reg)(lambda: greet(after))

    for c in range(PARTS):
        load(c).start()
    own_rows = pltpu.make_async_copy(obs, window.at[pl.ds(0, OWN), :], obs_sem)
    own_rows.start()
    own_piece = {
        r: pltpu.make_async_copy(obs.at[pl.ds(at, 128), :], hop, hop_sem)
        for r, at in ((0, 0), (7, OWN - 128))
    }
    for r in (0, 7):
        pl.when(b == r)(own_piece[r].start)

    weight[...] = jnp.zeros_like(weight)
    force[...] = jnp.zeros_like(force)
    for h in range(16):
        weight[h : h + 1, :] = prec[:, 128 * h : 128 * h + 128].astype(F32)
        innov[h : h + 1, :] = dep[:, 128 * h : 128 * h + 128].astype(F32)
    for side, first in ((0, 0), (1, 12)):
        rim_out[side, 0:4, :] = weight[first : first + 4, :]
        rim_out[side, 4:8, :] = innov[first : first + 4, :]

    perm = transpose_perm()

    def arrange(c, _):
        load(c).wait()

        def shuffle(g, _):
            rows = pl.ds(pl.multiple_of(g * 16, 16), 16)
            moved = dot(perm, stage[c, rows, :, :].reshape(256, WIDE)).astype(BF16)
            for i in range(16):
                to_rows = pl.ds(pl.multiple_of(i * SHARE + g * 16, 16), 16)
                send[c, to_rows, :] = moved[16 * i : 16 * i + 16, :]
            return _

        return lax.fori_loop(0, SHARE // 16, shuffle, _)

    lax.fori_loop(0, PARTS, arrange, 0)

    listed[...] = jnp.zeros_like(listed)
    live = tally[0, 0]

    def place(e, _):
        cols = pl.ds(pl.multiple_of(e * 512, 512), 512)
        entry = e * 512 + lax.broadcasted_iota(jnp.int32, (1, 512), 1)
        which, pos = code[:, cols], position[:, cols]
        row = jnp.where(which == 1, pos, jnp.where(which == 0, pos + RIM, pos + OWN + RIM))
        high, low = row // 128, row % 128
        value = jnp.where(entry < live, local[:, cols], 0.0)
        one = value.astype(BF16).astype(F32)
        two = (value - one).astype(BF16).astype(F32)
        three = value - one - two
        hot_low = (lax.broadcasted_iota(jnp.int32, (128, 512), 0) == low).astype(F32).astype(BF16)
        hot_high = lax.broadcasted_iota(jnp.int32, (32, 512), 0) == high
        for term in (three, two, one):
            part = jnp.where(hot_high, term, 0.0).astype(BF16)
            listed[...] += lax.dot_general(
                part, hot_low, (((1,), (1,)), ((), ())), preferred_element_type=F32
            )
        return _

    lax.fori_loop(0, LIST // 512, place, 0)
    weight[0:16, :] = weight[0:16, :] * listed[0:16, :]

    @pl.when(b % 7 != 0)
    def wait_inner():
        pl.semaphore_wait(barrier, NPEER + 8)

    @pl.when(b % 7 == 0)
    def wait_end():
        pl.semaphore_wait(barrier, NPEER + 9)

    small = [
        remote(rim_out.at[side], rim_in.at[1 - side], vec_ss.at[side], vec_rs.at[side], to)
        for side, to in ((0, before), (1, after))
    ]
    large = [
        remote(
            obs.at[pl.ds(at, RIM), :], window.at[pl.ds(OWN + RIM * (1 - side), RIM), :],
            rim_ss.at[side], rim_rs.at[side], (a, to),
        )
        for side, at, to in ((0, 0, (b + 7) % 8), (1, OWN - RIM, (b + 1) % 8))
    ]
    step_one = {
        r: [
            remote(obs.at[pl.ds(at + 128 * q, 128), :], hop, one_ss.at[n], one_rs, (a, 2 * q + r // 7))
            for n, q in enumerate(pieces)
        ]
        for r, at, pieces in ((0, 0, (1, 2, 3)), (7, OWN - RIM, (0, 1, 2)))
    }
    step_two = remote(hop, hop_two, two_ss, two_rs, partner)
    piece_rows = pl.ds(pl.multiple_of(OWN + RIM * odd + 128 * plane, 128), 128)
    step_three = remote(
        hop_two, window.at[piece_rows, :], three_ss, three_rs.at[plane], (a, 7 * odd)
    )
    last_step = {
        r: [
            remote(
                hop_two, window.at[pl.ds(at + 128 * q, 128), :], three_ss, three_rs.at[q], (a, r)
            )
            for q in pieces
        ]
        for r, at, pieces in ((0, OWN, (1, 2, 3)), (7, OWN + RIM, (0, 1, 2)))
    }

    for r in (0, 7):
        pl.when(b == r)(lambda r=r: [copy.start() for copy in step_one[r]] and None)
    for copy in small:
        copy.start()
    pl.when(b > 0)(large[0].start)
    pl.when(b < 7)(large[1].start)

    def send_part(c, _):
        for k in range(NPEER):
            forward(c, k).start()
        forward_own(c).start()
        return _

    send_part(0, 0)

    def rows_ready(first, last):
        force_rows = (weight[first:last, :] * innov[first:last, :]).astype(BF16).astype(F32)
        for h in range(first, last):
            force[0:1, 128 * h : 128 * h + 128] = force_rows[h - first : h - first + 1, :]

        def block(h, _):
            rows = pl.ds(pl.multiple_of(h * 128, 128), 128)
            w = jnp.broadcast_to(weight[pl.ds(h, 1), :], (128, 128)).T
            for j in range(8):
                cols = slice(128 * j, 128 * j + 128)
                tile = window[rows, cols]
                scaled[rows, cols] = (tile.astype(F32) * w).astype(BF16)
                turned[cols, rows] = tile.T
            return _

        lax.fori_loop(first, last, block, 0)

    def halves(body):
        def step(t, _):
            n = pl.multiple_of(t * 512, 512)
            body(n, pl.ds(n, 512))
            return _

        lax.fori_loop(0, 2, step, 0)

    def tiles(body):
        def step(t, _):
            m = pl.multiple_of(t * 128, 128)
            body(m, pl.ds(m, 128))
            return _

        lax.fori_loop(0, 8, step, 0)

    own_rows.wait()
    rows_ready(0, 16)
    gram[:, 0:512] = dot(turned[:, 0:OWN], scaled[0:OWN, 0:512])

    for r in (0, 7):
        pl.when(b == r)(own_piece[r].wait)
    pl.when(b % 7 != 0)(step_one[7][0].wait_recv)
    step_two.start()
    lax.fori_loop(1, PARTS, send_part, 0)

    gram[:, 512:1024] = dot(turned[:, 0:OWN], scaled[0:OWN, 512:1024])

    step_two.wait()

    @pl.when(b % 7 != 0)
    def pass_on():
        step_three.start()

    @pl.when(b % 7 == 0)
    def keep():
        window[piece_rows, :] = hop_two[...]

    for copy in small:
        copy.wait()
    pl.when(b < 7)(large[0].wait_recv)
    pl.when(b > 0)(large[1].wait_recv)
    for r in (0, 7):
        pl.when(b == r)(lambda r=r: [copy.wait_recv() for copy in last_step[r]] and None)
    for side in range(2):
        at = slice(16 + 4 * side, 20 + 4 * side)
        weight[at, :] = rim_in[side, 0:4, :] * listed[at, :]
        innov[at, :] = rim_in[side, 4:8, :]
    rows_ready(16, 24)

    high, low, s_high = (turned.at[:, 1024 * k : 1024 * k + 1024] for k in range(3))
    s_low, q_high, q_low = (scaled.at[1024 * k : 1024 * k + 1024, :] for k in range(3))

    def gram_rim(n, cols):
        ridge = jnp.where(eye_tile(0, n, 1024, 512), F32(RIDGE), 0.0)
        system = gram[:, cols] + dot(turned[:, OWN:WINDOW], scaled[OWN:WINDOW, cols]) + ridge
        gram[:, cols] = system
        high[:, cols], low[:, cols] = split(system)

    halves(gram_rim)
    drive = dot(force[...].astype(BF16), window[...])[0:1, :]

    def square(n, cols):
        root[:, cols] = dot(high[...], low[:, cols]) + dot(low[...], high[:, cols])
        root[:, cols] += dot(high[...], high[:, cols])

    halves(square)

    norm = row_times(root, jnp.ones((1, MEMBERS), F32), column)
    column[...] = column[...] / jnp.sqrt(norm)
    row = col_times(root, column)
    row = row / jnp.sqrt(total(row * row))
    norm = row_times(root, row, column)
    column[...] = column[...] / jnp.sqrt(norm)
    probe = jnp.concatenate(
        [column[128 * c : 128 * c + 128, :].T[0:1, :] for c in range(8)], axis=1
    )
    bound = total(probe * col_times(gram, column))
    inverse = 1.0 / bound

    def factors(m, rows):
        diagonal = eye_tile(m, 0, 128, 1024)
        unit = gram[rows, :] * inverse
        v = unit - jnp.where(diagonal, F32(MID), 0.0)
        s = root[rows, :] * (inverse * inverse) - 2 * MID * unit
        s += jnp.where(diagonal, F32(MID * MID), 0.0)
        s_high[rows, :], s_low[rows, :] = split(s)
        q_high[rows, :], q_low[rows, :] = split(A3 * v + A4 * s)
        root[rows, :] = jnp.where(diagonal, F32(A0), 0.0) + A1 * v + A2 * s

    tiles(factors)

    def quartic(n, cols):
        root[:, cols] += dot(s_high[...], q_low[:, cols]) + dot(s_low[...], q_high[:, cols])
        root[:, cols] += dot(s_high[...], q_high[:, cols])

    halves(quartic)

    to_column(drive, column)
    to_column(col_times(root, column), column)
    mean = col_times(root, column) * inverse
    size = jnp.sqrt((MEMBERS - 1) * inverse)

    def finish(m, rows):
        trans[rows, :] = (root[rows, :] * size + mean).astype(BF16)

    tiles(finish)

    def apply_part(c, _):
        for k in range(NPEER):
            forward(c, k).wait()
        forward_own(c).wait()

        def add(g, acc):
            rows = pl.ds(pl.multiple_of(g * 128, 128), 128)
            return acc + jnp.sum(recv[c, rows, :].astype(F32).reshape(16, 8, WIDE), axis=0)

        acc = lax.fori_loop(0, 8, add, jnp.zeros((8, WIDE), F32))
        center[...] = jnp.sum(acc, axis=0, keepdims=True) / MEMBERS

        def deviate(g, _):
            rows = pl.ds(pl.multiple_of(g * 128, 128), 128)
            dev[rows, :] = (recv[c, rows, :].astype(F32) - center[...]).astype(BF16)
            return _

        lax.fori_loop(0, 8, deviate, 0)
        send[c] = (center[...] + dot(trans[...], dev[...])).astype(BF16)
        for k in range(NPEER):
            backward(c, k).start()
        backward_own(c).start()
        return _

    lax.fori_loop(0, PARTS, apply_part, 0)

    pl.when(b > 0)(large[0].wait_send)
    pl.when(b < 7)(large[1].wait_send)
    for r in (0, 7):
        pl.when(b == r)(lambda r=r: [copy.wait_send() for copy in step_one[r]] and None)
    pl.when(b % 7 != 0)(step_three.wait_send)

    def drain(c, _):
        for k in range(NPEER):
            backward(c, k).wait()
        backward_own(c).wait()
        return _

    lax.fori_loop(0, PARTS, drain, 0)


def finish_kernel(moved, out, buffer, sem):
    def store(g):
        return pltpu.make_async_copy(buffer.at[g], out.at[pl.ds(16 * g, 16)], sem.at[g])

    perm = transpose_perm()
    for g in range(SHARE // 16):
        rows = moved[:, 16 * g : 16 * g + 16, :].reshape(256, GRID)
        buffer[g] = dot(perm, rows).astype(BF16).reshape(16, 16, GRID)
        store(g).start()
    for g in range(SHARE // 16):
        store(g).wait()


def local(
    prior_samples,
    measured_anomalies,
    measured_departure,
    measure_inverse_variance,
    measure_neighbour_code,
    measure_position,
    measure_tally,
    locality_weights,
):
    hbm = pl.BlockSpec(memory_space=pl.ANY)
    vmem = pl.BlockSpec(memory_space=pltpu.VMEM)
    smem = pl.BlockSpec(memory_space=pltpu.SMEM)
    dma = pltpu.SemaphoreType.DMA
    moved = pl.pallas_call(
        kernel,
        out_shape=pltpu.VMEM((GROUP, SHARE, GRID), BF16),
        in_specs=[hbm, hbm, vmem, vmem, vmem, vmem, smem, vmem],
        out_specs=vmem,
        scratch_shapes=[
            pltpu.VMEM((PARTS, SHARE, GROUP, WIDE), BF16),
            pltpu.VMEM((PARTS, MEMBERS, WIDE), BF16),
            pltpu.VMEM((PARTS, MEMBERS, WIDE), BF16),
            pltpu.VMEM((WINDOW, MEMBERS), BF16),
            pltpu.VMEM((MEMBERS, WINDOW), BF16),
            pltpu.VMEM((WINDOW, MEMBERS), BF16),
            pltpu.VMEM((MEMBERS, MEMBERS), F32),
            pltpu.VMEM((MEMBERS, MEMBERS), F32),
            pltpu.VMEM((MEMBERS, MEMBERS), BF16),
            pltpu.VMEM((MEMBERS, WIDE), BF16),
            pltpu.VMEM((128, MEMBERS), BF16),
            pltpu.VMEM((128, MEMBERS), BF16),
            pltpu.VMEM((32, 128), F32),
            pltpu.VMEM((24, 128), F32),
            pltpu.VMEM((24, 128), F32),
            pltpu.VMEM((MEMBERS, 128), F32),
            pltpu.VMEM((16, WINDOW), F32),
            pltpu.VMEM((2, 8, 128), F32),
            pltpu.VMEM((2, 8, 128), F32),
            pltpu.VMEM((1, WIDE), F32),
            dma((PARTS,)), dma((PARTS,)), dma, dma,
            dma((2,)), dma((2,)), dma((2,)), dma((2,)),
            dma((3,)), dma, dma, dma, dma, dma((4,)),
            dma((PARTS, NPEER)), dma((PARTS, NPEER)), dma((PARTS, NPEER)), dma((PARTS, NPEER)),
            dma((PARTS,)),
        ],
        compiler_params=pltpu.CompilerParams(
            collective_id=0, has_side_effects=True, vmem_limit_bytes=54 * 2**20
        ),
        cost_estimate=pl.CostEstimate(flops=24 * 10**9, bytes_accessed=12 * 2**20, transcendentals=0),
    )(
        prior_samples[:, :, 0, :],
        measured_anomalies[0, 0],
        measured_departure[0],
        measure_inverse_variance[0],
        measure_neighbour_code[0],
        measure_position[0],
        measure_tally,
        locality_weights[0],
    )
    out = pl.pallas_call(
        finish_kernel,
        out_shape=jax.ShapeDtypeStruct((SHARE, GROUP, GRID), BF16),
        in_specs=[vmem],
        out_specs=hbm,
        scratch_shapes=[pltpu.VMEM((SHARE // 16, 16, GROUP, GRID), BF16), dma((SHARE // 16,))],
        compiler_params=pltpu.CompilerParams(vmem_limit_bytes=20 * 2**20),
        cost_estimate=pl.CostEstimate(flops=10**9, bytes_accessed=8 * 2**20, transcendentals=0),
    )(moved)
    return out[:, :, None, :]


def solution(mesh):
    return jax.shard_map(
        local,
        mesh=mesh,
        in_specs=(
            P("mem", None, "reg", None),
            P("mem", "reg", None, None),
            P("mem", "reg", None),
            P("mem", "reg", None),
            P("mem", "reg", None),
            P("mem", "reg", None),
            P("mem", "reg"),
            P("mem", "reg", None),
        ),
        out_specs=P("mem", None, "reg", None),
        check_vma=False,
    )
```

time: 118 us -> 114 us (0.966)
  the two profiles are of different devices: /device:TPU:0 before, /device:TPU:64 now
where the time goes in v2:
time: 114 us; the launch traced here: 113 us
  Pallas kernels  113 us (99%)
    pallas_call x1, Pallas kernels, local(): pl.pallas_call(kernel, out_shape=pltpu.VMEM((GROUP, SHARE, GRID), BF16),...  110 us
    pallas_call x1, Pallas kernels, local(): pl.pallas_call(finish_kernel, out_shape=jax.ShapeDtypeStruct((SHARE, GROU...  2.39 us

profile of v2, /device:TPU:64, one launch (start us, length us, event | category | flops | bytes accessed | tf_op | source)
XLA Modules:
  0.0 113.4 jit_solution(2735013532981560125)
XLA Ops:
  0.7 110.2 %shard_map.82.moved = bf16[16,64,1920]{2,1,0:T(8,128)(2,1)S(1)} custom-call(bf16[64,16,1920]{2,1,0:T(8,128)(2,1)} %bitcast.11, bf16[2048,1024]{1,0:T(8,128)(2,1)} %bitcast.10, bf16[1,2048]{1,0:T(2,128)(2,1)} %bitcast.15, bf16[1,2048]{1,0:T(2,128)(2,1)} %bitcast.16, s32[1,2560]{1,0:T(1,128)} %bitcast.12, s32[1,2560]{1,0:T(1,128)} %bitcast.13, ...), custom_call_target="tpu_custom_call" | custom-call | flops 24000000000 | bytes 12582912 | tf_op jit(solution)/shard_map/pallas_call | solution.py:482
  110.9 2.4 %shard_map.83 = bf16[64,16,1920]{2,1,0:T(8,128)(2,1)} custom-call(bf16[16,64,1920]{2,1,0:T(8,128)(2,1)S(1)} %shard_map.82.moved), custom_call_target="tpu_custom_call" | custom-call | flops 1000000000 | bytes 8388608 | tf_op jit(solution)/shard_map/pallas_call | solution.py:528

commit v3 on v2

--- a/solution.py
+++ b/solution.py
@@ -30,6 +30,7 @@
     (2, 2),
 )
 NPEER = len(PEERS)
+FEW = 15
 
 MID = 0.5
 A0 = (36 - 39 * MID + 27 * MID**2 - 9 * MID**3 + MID**4) / 16
@@ -203,32 +204,7 @@
 
         return lax.fori_loop(0, SHARE // 16, shuffle, _)
 
-    lax.fori_loop(0, PARTS, arrange, 0)
-
-    listed[...] = jnp.zeros_like(listed)
-    live = tally[0, 0]
-
-    def place(e, _):
-        cols = pl.ds(pl.multiple_of(e * 512, 512), 512)
-        entry = e * 512 + lax.broadcasted_iota(jnp.int32, (1, 512), 1)
-        which, pos = code[:, cols], position[:, cols]
-        row = jnp.where(which == 1, pos, jnp.where(which == 0, pos + RIM, pos + OWN + RIM))
-        high, low = row // 128, row % 128
-        value = jnp.where(entry < live, local[:, cols], 0.0)
-        one = value.astype(BF16).astype(F32)
-        two = (value - one).astype(BF16).astype(F32)
-        three = value - one - two
-        hot_low = (lax.broadcasted_iota(jnp.int32, (128, 512), 0) == low).astype(F32).astype(BF16)
-        hot_high = lax.broadcasted_iota(jnp.int32, (32, 512), 0) == high
-        for term in (three, two, one):
-            part = jnp.where(hot_high, term, 0.0).astype(BF16)
-            listed[...] += lax.dot_general(
-                part, hot_low, (((1,), (1,)), ((), ())), preferred_element_type=F32
-            )
-        return _
-
-    lax.fori_loop(0, LIST // 512, place, 0)
-    weight[0:16, :] = weight[0:16, :] * listed[0:16, :]
+    arrange(0, 0)
 
     @pl.when(b % 7 != 0)
     def wait_inner():
@@ -275,8 +251,38 @@
         pl.when(b == r)(lambda r=r: [copy.start() for copy in step_one[r]] and None)
     for copy in small:
         copy.start()
-    pl.when(b > 0)(large[0].start)
-    pl.when(b < 7)(large[1].start)
+
+    pl.when(odd == 1)(large[0].start)
+    pl.when(odd == 0)(large[1].start)
+
+    for k in range(FEW):
+        forward(0, k).start()
+    forward_own(0).start()
+    lax.fori_loop(1, PARTS, arrange, 0)
+    listed[...] = jnp.zeros_like(listed)
+    live = tally[0, 0]
+
+    def place(e, _):
+        cols = pl.ds(pl.multiple_of(e * 512, 512), 512)
+        entry = e * 512 + lax.broadcasted_iota(jnp.int32, (1, 512), 1)
+        which, pos = code[:, cols], position[:, cols]
+        row = jnp.where(which == 1, pos, jnp.where(which == 0, pos + RIM, pos + OWN + RIM))
+        high, low = row // 128, row % 128
+        value = jnp.where(entry < live, local[:, cols], 0.0)
+        one = value.astype(BF16).astype(F32)
+        two = (value - one).astype(BF16).astype(F32)
+        three = value - one - two
+        hot_low = (lax.broadcasted_iota(jnp.int32, (128, 512), 0) == low).astype(F32).astype(BF16)
+        hot_high = lax.broadcasted_iota(jnp.int32, (32, 512), 0) == high
+        for term in (three, two, one):
+            part = jnp.where(hot_high, term, 0.0).astype(BF16)
+            listed[...] += lax.dot_general(
+                part, hot_low, (((1,), (1,)), ((), ())), preferred_element_type=F32
+            )
+        return _
+
+    lax.fori_loop(0, LIST // 512, place, 0)
+    weight[0:16, :] = weight[0:16, :] * listed[0:16, :]
 
     def send_part(c, _):
         for k in range(NPEER):
@@ -284,7 +290,15 @@
         forward_own(c).start()
         return _
 
-    send_part(0, 0)
+    for r in (0, 7):
+        pl.when(b == r)(own_piece[r].wait)
+    pl.when(b % 7 != 0)(step_one[7][0].wait_recv)
+    step_two.start()
+    pl.when((odd == 0) & (b > 0))(large[0].start)
+    pl.when((odd == 1) & (b < 7))(large[1].start)
+    for k in range(FEW, NPEER):
+        forward(0, k).start()
+    lax.fori_loop(1, PARTS, send_part, 0)
 
     def rows_ready(first, last):
         force_rows = (weight[first:last, :] * innov[first:last, :]).astype(BF16).astype(F32)
@@ -321,15 +335,13 @@
 
     own_rows.wait()
     rows_ready(0, 16)
-    gram[:, 0:512] = dot(turned[:, 0:OWN], scaled[0:OWN, 0:512])
-
-    for r in (0, 7):
-        pl.when(b == r)(own_piece[r].wait)
-    pl.when(b % 7 != 0)(step_one[7][0].wait_recv)
-    step_two.start()
-    lax.fori_loop(1, PARTS, send_part, 0)
-
-    gram[:, 512:1024] = dot(turned[:, 0:OWN], scaled[0:OWN, 512:1024])
+
+
+    def gram_own(n, cols):
+        gram[:, cols] = dot(turned[:, 0:OWN], scaled[0:OWN, cols])
+
+    halves(gram_own)
+    drive = dot(force[:, 0:OWN].astype(BF16), window[0:OWN, :])
 
     step_two.wait()
 
@@ -353,8 +365,8 @@
         innov[at, :] = rim_in[side, 4:8, :]
     rows_ready(16, 24)
 
-    high, low, s_high = (turned.at[:, 1024 * k : 1024 * k + 1024] for k in range(3))
-    s_low, q_high, q_low = (scaled.at[1024 * k : 1024 * k + 1024, :] for k in range(3))
+    high, low, square_bf = (turned.at[:, 1024 * k : 1024 * k + 1024] for k in range(3))
+    cubic_bf = scaled.at[0:1024, :]
 
     def gram_rim(n, cols):
         ridge = jnp.where(eye_tile(0, n, 1024, 512), F32(RIDGE), 0.0)
@@ -363,7 +375,7 @@
         high[:, cols], low[:, cols] = split(system)
 
     halves(gram_rim)
-    drive = dot(force[...].astype(BF16), window[...])[0:1, :]
+    drive += dot(force[:, OWN:WINDOW].astype(BF16), window[OWN:WINDOW, :])
 
     def square(n, cols):
         root[:, cols] = dot(high[...], low[:, cols]) + dot(low[...], high[:, cols])
@@ -389,19 +401,18 @@
         v = unit - jnp.where(diagonal, F32(MID), 0.0)
         s = root[rows, :] * (inverse * inverse) - 2 * MID * unit
         s += jnp.where(diagonal, F32(MID * MID), 0.0)
-        s_high[rows, :], s_low[rows, :] = split(s)
-        q_high[rows, :], q_low[rows, :] = split(A3 * v + A4 * s)
+        square_bf[rows, :] = s.astype(BF16)
+        cubic_bf[rows, :] = (A3 * v + A4 * s).astype(BF16)
         root[rows, :] = jnp.where(diagonal, F32(A0), 0.0) + A1 * v + A2 * s
 
     tiles(factors)
 
     def quartic(n, cols):
-        root[:, cols] += dot(s_high[...], q_low[:, cols]) + dot(s_low[...], q_high[:, cols])
-        root[:, cols] += dot(s_high[...], q_high[:, cols])
+        root[:, cols] += dot(square_bf[...], cubic_bf[:, cols])
 
     halves(quartic)
 
-    to_column(drive, column)
+    to_column(drive[0:1, :], column)
     to_column(col_times(root, column), column)
     mean = col_times(root, column) * inverse
     size = jnp.sqrt((MEMBERS - 1) * inverse)

time: 114 us -> 106 us (0.930)
  the two profiles are of different devices: /device:TPU:64 before, /device:TPU:0 now
where the time goes in v3:
time: 106 us; the launch traced here: 105 us
  Pallas kernels  105 us (99%)
    pallas_call x1, Pallas kernels, local(): pl.pallas_call(kernel, out_shape=pltpu.VMEM((GROUP, SHARE, GRID), BF16),...  102 us
    pallas_call x1, Pallas kernels, local(): pl.pallas_call(finish_kernel, out_shape=jax.ShapeDtypeStruct((SHARE, GROU...  2.39 us

profile of v3, /device:TPU:0, one launch (start us, length us, event | category | flops | bytes accessed | tf_op | source)
XLA Modules:
  0.0 105.2 jit_solution(13680895405107143357)
XLA Ops:
  0.7 102.2 %shard_map.82.moved = bf16[16,64,1920]{2,1,0:T(8,128)(2,1)S(1)} custom-call(bf16[64,16,1920]{2,1,0:T(8,128)(2,1)} %bitcast.11, bf16[2048,1024]{1,0:T(8,128)(2,1)} %bitcast.10, bf16[1,2048]{1,0:T(2,128)(2,1)} %bitcast.15, bf16[1,2048]{1,0:T(2,128)(2,1)} %bitcast.16, s32[1,2560]{1,0:T(1,128)} %bitcast.12, s32[1,2560]{1,0:T(1,128)} %bitcast.13, ...), custom_call_target="tpu_custom_call" | custom-call | flops 24000000000 | bytes 12582912 | tf_op jit(solution)/shard_map/pallas_call | solution.py:493
  102.8 2.4 %shard_map.83 = bf16[64,16,1920]{2,1,0:T(8,128)(2,1)} custom-call(bf16[16,64,1920]{2,1,0:T(8,128)(2,1)S(1)} %shard_map.82.moved), custom_call_target="tpu_custom_call" | custom-call | flops 1000000000 | bytes 8388608 | tf_op jit(solution)/shard_map/pallas_call | solution.py:539

commit v4 on v3

--- a/solution.py
+++ b/solution.py
@@ -98,11 +98,11 @@
 
 
 def kernel(
-    prior, obs, dep, prec, code, position, tally, local,
+    prior, obs, dep_hbm, prec_hbm, code_hbm, position_hbm, tally, local_hbm,
     out,
-    stage, send, recv, window, turned, scaled, gram, root, trans, dev, hop, hop_two,
+    dep, prec, code, position, local, stage, send, recv, window, turned, scaled, gram, root, trans, dev, hop, hop_two,
     listed, weight, innov, column, force, rim_out, rim_in, center,
-    load_sem, own_sem, obs_sem, hop_sem, rim_ss, rim_rs, vec_ss, vec_rs,
+    vector_sem, load_sem, own_sem, obs_sem, hop_sem, rim_ss, rim_rs, vec_ss, vec_rs,
     one_ss, one_rs, two_ss, two_rs, three_ss, three_rs, fs, fr, bs, br, back_sem,
 ):
     a, b = lax.axis_index("mem"), lax.axis_index("reg")
@@ -180,14 +180,15 @@
     for r in (0, 7):
         pl.when(b == r)(own_piece[r].start)
 
-    weight[...] = jnp.zeros_like(weight)
-    force[...] = jnp.zeros_like(force)
-    for h in range(16):
-        weight[h : h + 1, :] = prec[:, 128 * h : 128 * h + 128].astype(F32)
-        innov[h : h + 1, :] = dep[:, 128 * h : 128 * h + 128].astype(F32)
-    for side, first in ((0, 0), (1, 12)):
-        rim_out[side, 0:4, :] = weight[first : first + 4, :]
-        rim_out[side, 4:8, :] = innov[first : first + 4, :]
+    vectors = [
+        pltpu.make_async_copy(source, target, vector_sem.at[n])
+        for n, (source, target) in enumerate((
+            (dep_hbm, dep), (prec_hbm, prec), (code_hbm, code),
+            (position_hbm, position), (local_hbm, local),
+        ))
+    ]
+    for copy in vectors:
+        copy.start()
 
     perm = transpose_perm()
 
@@ -249,15 +250,26 @@
 
     for r in (0, 7):
         pl.when(b == r)(lambda r=r: [copy.start() for copy in step_one[r]] and None)
-    for copy in small:
-        copy.start()
-
-    pl.when(odd == 1)(large[0].start)
-    pl.when(odd == 0)(large[1].start)
-
     for k in range(FEW):
         forward(0, k).start()
     forward_own(0).start()
+
+    pl.when(odd == 1)(large[0].start)
+    pl.when(odd == 0)(large[1].start)
+
+    for copy in vectors:
+        copy.wait()
+    weight[...] = jnp.zeros_like(weight)
+    force[...] = jnp.zeros_like(force)
+    for h in range(16):
+        weight[h : h + 1, :] = prec[:, 128 * h : 128 * h + 128].astype(F32)
+        innov[h : h + 1, :] = dep[:, 128 * h : 128 * h + 128].astype(F32)
+    for side, first in ((0, 0), (1, 12)):
+        rim_out[side, 0:4, :] = weight[first : first + 4, :]
+        rim_out[side, 4:8, :] = innov[first : first + 4, :]
+    for copy in small:
+        copy.start()
+
     lax.fori_loop(1, PARTS, arrange, 0)
     listed[...] = jnp.zeros_like(listed)
     live = tally[0, 0]
@@ -488,14 +500,18 @@
 ):
     hbm = pl.BlockSpec(memory_space=pl.ANY)
     vmem = pl.BlockSpec(memory_space=pltpu.VMEM)
-    smem = pl.BlockSpec(memory_space=pltpu.SMEM)
     dma = pltpu.SemaphoreType.DMA
     moved = pl.pallas_call(
         kernel,
         out_shape=pltpu.VMEM((GROUP, SHARE, GRID), BF16),
-        in_specs=[hbm, hbm, vmem, vmem, vmem, vmem, smem, vmem],
+        in_specs=[hbm] * 6 + [pl.BlockSpec(memory_space=pltpu.SMEM), hbm],
         out_specs=vmem,
         scratch_shapes=[
+            pltpu.VMEM((1, OWN), BF16),
+            pltpu.VMEM((1, OWN), BF16),
+            pltpu.VMEM((1, LIST), jnp.int32),
+            pltpu.VMEM((1, LIST), jnp.int32),
+            pltpu.VMEM((1, LIST), F32),
             pltpu.VMEM((PARTS, SHARE, GROUP, WIDE), BF16),
             pltpu.VMEM((PARTS, MEMBERS, WIDE), BF16),
             pltpu.VMEM((PARTS, MEMBERS, WIDE), BF16),
@@ -516,7 +532,7 @@
             pltpu.VMEM((2, 8, 128), F32),
             pltpu.VMEM((2, 8, 128), F32),
             pltpu.VMEM((1, WIDE), F32),
-            dma((PARTS,)), dma((PARTS,)), dma, dma,
+            dma((5,)), dma((PARTS,)), dma((PARTS,)), dma, dma,
             dma((2,)), dma((2,)), dma((2,)), dma((2,)),
             dma((3,)), dma, dma, dma, dma, dma((4,)),
             dma((PARTS, NPEER)), dma((PARTS, NPEER)), dma((PARTS, NPEER)), dma((PARTS, NPEER)),

time: 106 us -> 105 us (level)
  no operation moved by 1% of the time
where the time goes in v4:
time: 105 us
  Pallas kernels  104 us (99%)
    pallas_call x1, Pallas kernels, local(): pl.pallas_call(kernel, out_shape=pltpu.VMEM((GROUP, SHARE, GRID), BF16),...  102 us
    pallas_call x1, Pallas kernels, local(): pl.pallas_call(finish_kernel, out_shape=jax.ShapeDtypeStruct((SHARE, GROU...  2.39 us

profile of v4, /device:TPU:0, one launch (start us, length us, event | category | flops | bytes accessed | tf_op | source)
XLA Modules:
  0.0 104.6 jit_solution(3037224408196704041)
XLA Ops:
  0.7 101.6 %shard_map.82.moved = bf16[16,64,1920]{2,1,0:T(8,128)(2,1)S(1)} custom-call(bf16[64,16,1920]{2,1,0:T(8,128)(2,1)} %bitcast.11, bf16[2048,1024]{1,0:T(8,128)(2,1)} %bitcast.10, bf16[1,2048]{1,0:T(2,128)(2,1)} %bitcast.15, bf16[1,2048]{1,0:T(2,128)(2,1)} %bitcast.16, s32[1,2560]{1,0:T(1,128)} %bitcast.12, s32[1,2560]{1,0:T(1,128)} %bitcast.13, ...), custom_call_target="tpu_custom_call" | custom-call | flops 24000000000 | bytes 12582912 | tf_op jit(solution)/shard_map/pallas_call | solution.py:504
  102.2 2.4 %shard_map.83 = bf16[64,16,1920]{2,1,0:T(8,128)(2,1)} custom-call(bf16[16,64,1920]{2,1,0:T(8,128)(2,1)S(1)} %shard_map.82.moved), custom_call_target="tpu_custom_call" | custom-call | flops 1000000000 | bytes 8388608 | tf_op jit(solution)/shard_map/pallas_call | solution.py:555

commit v5 on v4

--- a/solution.py
+++ b/solution.py
@@ -453,7 +453,7 @@
 
         lax.fori_loop(0, 8, deviate, 0)
         send[c] = (center[...] + dot(trans[...], dev[...])).astype(BF16)
-        for k in range(NPEER):
+        for k in (14, 0, 10, 1, 11, 2, 12, 3, 13, 4, 8, 5, 9, 6, 7):
             backward(c, k).start()
         backward_own(c).start()
         return _

time: 105 us -> 105 us (level)
  no operation moved by 1% of the time
where the time goes in v5:
time: 105 us
  Pallas kernels  104 us (99%)
    pallas_call x1, Pallas kernels, local(): pl.pallas_call(kernel, out_shape=pltpu.VMEM((GROUP, SHARE, GRID), BF16),...  101 us
    pallas_call x1, Pallas kernels, local(): pl.pallas_call(finish_kernel, out_shape=jax.ShapeDtypeStruct((SHARE, GROU...  2.39 us

profile of v5, /device:TPU:0, one launch (start us, length us, event | category | flops | bytes accessed | tf_op | source)
XLA Modules:
  0.0 104.5 jit_solution(2859131223268589218)
XLA Ops:
  0.7 101.5 %shard_map.82.moved = bf16[16,64,1920]{2,1,0:T(8,128)(2,1)S(1)} custom-call(bf16[64,16,1920]{2,1,0:T(8,128)(2,1)} %bitcast.11, bf16[2048,1024]{1,0:T(8,128)(2,1)} %bitcast.10, bf16[1,2048]{1,0:T(2,128)(2,1)} %bitcast.15, bf16[1,2048]{1,0:T(2,128)(2,1)} %bitcast.16, s32[1,2560]{1,0:T(1,128)} %bitcast.12, s32[1,2560]{1,0:T(1,128)} %bitcast.13, ...), custom_call_target="tpu_custom_call" | custom-call | flops 24000000000 | bytes 12582912 | tf_op jit(solution)/shard_map/pallas_call | solution.py:504
  102.1 2.4 %shard_map.83 = bf16[64,16,1920]{2,1,0:T(8,128)(2,1)} custom-call(bf16[16,64,1920]{2,1,0:T(8,128)(2,1)S(1)} %shard_map.82.moved), custom_call_target="tpu_custom_call" | custom-call | flops 1000000000 | bytes 8388608 | tf_op jit(solution)/shard_map/pallas_call | solution.py:555
